TPU v7x, 32 devices: a whole 2x2x4 slice. The times are simulated.
32 devices in a mesh: grp: 4 (over y, x), ctx: 8 (over z, core).
Axes of the slice: x: 2, y: 2, z: 4, core: 2. Of those that a mesh axis runs over, the one named last changes fastest.
Arguments:
- queries: bfloat16 [16384, 1024], P(('grp', 'ctx')), may hold values from -6 to 6
- keys: bfloat16 [16384, 1024], P(('grp', 'ctx')), may hold values from -6 to 6
- values: bfloat16 [16384, 1024], P(('grp', 'ctx')), may hold values from -6 to 6
- level_weights: float32 [13, 8, 16384], P(None, None, ('grp', 'ctx')), may hold values from 0.1 to 1.5
Outputs:
- attended: bfloat16 [16384, 1024], P(('grp', 'ctx'))
All inputs are finite; a program needn't handle non-finite values.
Results may differ from a plain program's by a relative error of at most 0.0095.
Values may be sent and summed in bfloat16 or wider, within the bound.
A program may use at most 64 MiB of HBM per device.

v0:
```python
import math

import jax
import jax.numpy as jnp
from jax import lax
from jax.sharding import PartitionSpec as P

DK = 128
STRETCH = 64


def from_partner(block, axis, stride):
    count = lax.axis_size(axis)
    route = []
    for low in range(count):
        high = low | 1 << stride
        if high != low and high < count:
            route += [(low, high), (high, low)]
    return lax.ppermute(block, axis, route)


def level_factor(level_num):
    token_count = STRETCH if level_num == 0 else STRETCH * 2 ** (level_num - 1)
    return 1.0 / math.sqrt(DK * token_count)


def local_part(query_matrix, key_matrix, value_matrix, level_rows):
    row_count = query_matrix.shape[0]
    local_bits = (row_count // STRETCH).bit_length() - 1
    position = jnp.arange(row_count, dtype=jnp.int32)
    block_ids = position // STRETCH
    stretch_xor = jnp.bitwise_xor(block_ids[:, None], block_ids[None, :])
    level_ids = jnp.zeros((row_count, row_count), jnp.int32)
    for bit_num in range(local_bits):
        level_ids = level_ids + (stretch_xor >= 2**bit_num).astype(jnp.int32)
    causal = position[:, None] >= position[None, :]
    weight = jnp.zeros((level_rows.shape[1], row_count, row_count), jnp.float32)
    for level_num in range(local_bits + 1):
        picked = jnp.logical_and(level_ids == level_num, causal)
        weight = weight + jnp.where(
            picked[None], (level_rows[level_num] * level_factor(level_num))[:, :, None], 0.0
        )
    scores = jnp.einsum(
        "thk,shk->hts", query_matrix, key_matrix, preferred_element_type=jnp.float32
    )
    weighted = (scores * weight).astype(jnp.bfloat16)
    return jnp.einsum("hts,shv->thv", weighted, value_matrix, preferred_element_type=jnp.float32)


def on_device(queries, keys, values, level_weights):
    row_count = queries.shape[0]
    head_count = level_weights.shape[1]
    head_width = queries.shape[1] // head_count
    query_matrix = queries.reshape(row_count, head_count, head_width)
    key_matrix = keys.reshape(row_count, head_count, head_width)
    value_matrix = values.reshape(row_count, head_count, head_width)
    local_bits = (row_count // STRETCH).bit_length() - 1
    ctx_bits = lax.axis_size("ctx").bit_length() - 1
    grp_bits = lax.axis_size("grp").bit_length() - 1
    ctx_index = lax.axis_index("ctx")
    grp_index = lax.axis_index("grp")
    kv_state = jnp.einsum(
        "pdx,pdo->dxo", key_matrix, value_matrix, preferred_element_type=jnp.float32
    ).astype(jnp.bfloat16)
    siblings = []
    running = kv_state.astype(jnp.float32)
    for bit_num in range(ctx_bits):
        partner = from_partner(running, "ctx", bit_num)
        left_half = jnp.right_shift(ctx_index, bit_num) % 2 == 1
        siblings.append(jnp.where(left_half, partner, 0.0))
        running = running + partner
    group_state = running.astype(jnp.bfloat16)
    running = group_state.astype(jnp.float32)
    for bit_num in range(grp_bits):
        partner = from_partner(running.astype(jnp.bfloat16), "grp", bit_num).astype(running.dtype)
        left_half = jnp.right_shift(grp_index, bit_num) % 2 == 1
        siblings.append(jnp.where(left_half, partner, 0.0))
        if bit_num + 1 < grp_bits:
            running = running + partner
    attended = local_part(query_matrix, key_matrix, value_matrix, level_weights)
    for bit_num in range(len(siblings)):
        level_num = 1 + local_bits + bit_num
        level_scale = (level_weights[level_num] * level_factor(level_num)).T
        outer_product = jnp.einsum(
            "ryl,ylf->ryf",
            query_matrix,
            siblings[bit_num].astype(jnp.bfloat16),
            preferred_element_type=jnp.float32,
        )
        attended = attended + outer_product * level_scale[:, :, None]
    return attended.reshape(row_count, head_count * head_width).astype(jnp.bfloat16)


def solution(mesh):
    return jax.shard_map(
        on_device,
        mesh=mesh,
        in_specs=(
            P(("grp", "ctx"), None),
            P(("grp", "ctx"), None),
            P(("grp", "ctx"), None),
            P(None, None, ("grp", "ctx")),
        ),
        out_specs=P(("grp", "ctx"), None),
        check_vma=False,
    )
```

profile of v0, /device:TPU:24, one launch (start us, length us, event | category | flops | bytes accessed | tf_op | source)
XLA Modules:
  0.0 64.3 jit_solution(6117273187700237023)
XLA Ops:
  0.0 1.6 %copy.24 = bf16[512,1024]{0,1:T(8,128)(2,1)S(1)} copy(bf16[512,1024]{1,0:T(8,128)(2,1)} %param.5) | data formatting | bytes 2097152 | tf_op jit(solution)/shard_map/reshape | solution.py:55
  1.6 1.7 %fusion.13 = f32[8,128,128]{2,1,0:T(8,128)S(1)} fusion(bf16[512,8,128]{0,2,1:T(8,128)(2,1)S(1)} %bitcast.111, bf16[512,1024]{1,0:T(8,128)(2,1)} %param.6), kind=kOutput, calls=%fused_computation.22 | convolution fusion | flops 134479872 | bytes 2621440 | tf_op jit(solution)/shard_map/pdx,pdo->dxo/dot_general | solution.py:62
  3.3 0.1 collective-permute-start
  3.5 1.7 %fusion.30 = (pred[512,512]{1,0:T(8,128)(4,1)S(1)}, pred[512,512]{1,0:T(8,128)(4,1)}, pred[512,512]{1,0:T(8,128)(4,1)}, pred[512,512]{1,0:T(8,128)(4,1)}) fusion(s32[512]{0:T(512)S(1)} %add_select_fusion), kind=kLoop, calls=%fused_computation.39 | loop fusion | flops 4718592 | bytes 1050624 | tf_op jit(solution)/shard_map/and | solution.py:39
  5.2 0.2 collective-permute-done
  5.4 1.1 %add.113 = f32[8,128,128]{2,1,0:T(8,128)S(1)} add(f32[8,128,128]{2,1,0:T(8,128)S(1)} %fusion.13, f32[8,128,128]{2,1,0:T(8,128)} %collective-permute-done) | non-fusion elementwise | flops 131072 | bytes 1572864 | tf_op jit(solution)/shard_map/add | solution.py:71
  6.5 0.5 collective-permute-start.1
  7.0 8.0 %fusion = f32[8,512,128]{1,2,0:T(8,128)} fusion(f32[8,512]{1,0:T(8,128)S(1)} %get-tuple-element.8, f32[8,512]{1,0:T(8,128)S(1)} %get-tuple-element.9, f32[8,512]{1,0:T(8,128)S(1)} %get-tuple-element.10, f32[8,512]{1,0:T(8,128)S(1)} %get-tuple-element.11, pred[512,512]{1,0:T(8,128)(4,1)} %get-tuple-element.15, pred[512,512]{1,0:T(8,128)(4,1)} %get-tuple-element.17, ...), kind=kOutput, calls=%fused_computation.1 | convolution fusion | flops 1092616192 | bytes 6356992 | tf_op jit(solution)/shard_map/hts,shv->thv/dot_general | solution.py:47
  15.0 5.7 %collective-permute-done.1 = f32[8,128,128]{2,1,0:T(8,128)S(1)} collective-permute-done((f32[8,128,128]{2,1,0:T(8,128)S(1)}, f32[8,128,128]{2,1,0:T(8,128)S(1)}, u32[]{:S(2)}, u32[]{:S(2)}) %collective-permute-start.1) | collective-permute-done | bytes 524320 | tf_op jit(solution)/shard_map/ppermute | solution.py:19
  20.6 0.1 add.116
  20.7 0.4 collective-permute-start.2
  21.1 0.5 fusion.25
  21.6 0.5 fusion.21
  22.1 24.0 %collective-permute-done.2 = f32[8,128,128]{2,1,0:T(8,128)S(1)} collective-permute-done((f32[8,128,128]{2,1,0:T(8,128)S(1)}, f32[8,128,128]{2,1,0:T(8,128)S(1)}, u32[]{:S(2)}, u32[]{:S(2)}) %collective-permute-start.2) | collective-permute-done | bytes 524320 | tf_op jit(solution)/shard_map/ppermute | solution.py:19
  46.1 0.1 add_convert_fusion
  46.1 1.6 %collective-permute-start.3 = (bf16[8,128,128]{2,1,0:T(8,128)(2,1)S(1)}, bf16[8,128,128]{2,1,0:T(8,128)(2,1)S(1)}, u32[]{:S(2)}, u32[]{:S(2)}) collective-permute-start(bf16[8,128,128]{2,1,0:T(8,128)(2,1)S(1)} %add_convert_fusion), channel_id=1, source_target_pairs={{0,8},{8,0},{16,24},{24,16},{1,9},{9,1},{17,25},{25,17},{2,10},{10... | collective-permute-start | bytes 786440 | tf_op jit(solution)/shard_map/ppermute | solution.py:19
  47.7 0.5 fusion.19
  48.2 6.2 %collective-permute-done.3 = bf16[8,128,128]{2,1,0:T(8,128)(2,1)S(1)} collective-permute-done((bf16[8,128,128]{2,1,0:T(8,128)(2,1)S(1)}, bf16[8,128,128]{2,1,0:T(8,128)(2,1)S(1)}, u32[]{:S(2)}, u32[]{:S(2)}) %collective-permute-start.3) | collective-permute-done | bytes 262176 | tf_op jit(solution)/shard_map/ppermute | solution.py:19
  54.4 0.1 fusion.38
  54.5 1.6 %collective-permute-start.4 = (bf16[8,128,128]{2,1,0:T(8,128)(2,1)S(1)}, bf16[8,128,128]{2,1,0:T(8,128)(2,1)S(1)}, u32[]{:S(2)}, u32[]{:S(2)}) collective-permute-start(bf16[8,128,128]{2,1,0:T(8,128)(2,1)S(1)} %fusion.38), channel_id=1, source_target_pairs={{0,16},{16,0},{8,24},{24,8},{1,17},{17,1},{9,25},{25,9},{2,18},{18... | collective-permute-start | bytes 786440 | tf_op jit(solution)/shard_map/ppermute | solution.py:19
  56.1 0.5 fusion.17
  56.6 5.4 %collective-permute-done.4 = bf16[8,128,128]{2,1,0:T(8,128)(2,1)S(1)} collective-permute-done((bf16[8,128,128]{2,1,0:T(8,128)(2,1)S(1)}, bf16[8,128,128]{2,1,0:T(8,128)(2,1)S(1)}, u32[]{:S(2)}, u32[]{:S(2)}) %collective-permute-start.4) | collective-permute-done | bytes 262176 | tf_op jit(solution)/shard_map/ppermute | solution.py:19
  61.9 1.0 %fusion.8 = bf16[512,8,128]{0,2,1:T(8,128)(2,1)S(1)} fusion(f32[8,128,512]{2,1,0:T(8,128)S(1)} %fusion.17, f32[8,128,512]{2,1,0:T(8,128)S(1)} %fusion.19, f32[8,128,512]{2,1,0:T(8,128)S(1)} %fusion.21, f32[8,128,512]{2,1,0:T(8,128)S(1)} %fusion.25, f32[8,512,128]{1,2,0:T(8,128)S(1)} %copy-done.1, f32[512,8]{0,1:T(8,128)S(1)} %get-tuple-element.12, ...), kind=kOutput, calls=%fused_computation.9 | convolution fusion | flops 140378112 | bytes 12926977 | tf_op jit(solution)/shard_map/ryl,ylf->ryf/dot_general | solution.py:84
  62.9 1.3 %copy.18 = bf16[512,1024]{1,0:T(8,128)(2,1)} copy(bf16[512,1024]{0,1:T(8,128)(2,1)S(1)} %bitcast.110) | data formatting | bytes 2097152 | tf_op jit(solution)/shard_map/convert_element_type | solution.py:91
  (8 shorter events, 0.0 us)
Async XLA Ops:
  0.0 7.0 %copy-start = (bf16[512,1024]{1,0:T(8,128)(2,1)S(1)}, bf16[512,1024]{1,0:T(8,128)(2,1)}, u32[]{:S(2)}) copy-start(bf16[512,1024]{1,0:T(8,128)(2,1)} %param.4) | copy-start | bytes 3145732
  0.0 3.4 %copy-start.2 = (f32[13,8,512]{2,1,0:T(8,128)S(1)}, f32[13,8,512]{2,1,0:T(8,128)}, u32[]{:S(2)}) copy-start(f32[13,8,512]{2,1,0:T(8,128)} %param.7) | copy-start | bytes 638980
  3.3 2.1 %collective-permute-start = (f32[8,128,128]{2,1,0:T(8,128)S(1)}, f32[8,128,128]{2,1,0:T(8,128)}, u32[]{:S(2)}, u32[]{:S(2)}) collective-permute-start(f32[8,128,128]{2,1,0:T(8,128)S(1)} %fusion.13), channel_id=1, source_target_pairs={{0,1},{1,0},{2,3},{3,2},{4,5},{5,4},{6,7},{7,6},{8,9},{9,8},{10,11... | collective-permute-start | bytes 1572872 | tf_op jit(solution)/shard_map/ppermute | solution.py:19
  6.5 14.1 %collective-permute-start.1 = (f32[8,128,128]{2,1,0:T(8,128)S(1)}, f32[8,128,128]{2,1,0:T(8,128)S(1)}, u32[]{:S(2)}, u32[]{:S(2)}) collective-permute-start(f32[8,128,128]{2,1,0:T(8,128)S(1)} %add.113), channel_id=1, source_target_pairs={{0,2},{2,0},{1,3},{3,1},{4,6},{6,4},{5,7},{7,5},{8,10},{10,8},{9,1... | collective-permute-start | bytes 1572872 | tf_op jit(solution)/shard_map/ppermute | solution.py:19
  20.7 25.3 %collective-permute-start.2 = (f32[8,128,128]{2,1,0:T(8,128)S(1)}, f32[8,128,128]{2,1,0:T(8,128)S(1)}, u32[]{:S(2)}, u32[]{:S(2)}) collective-permute-start(f32[8,128,128]{2,1,0:T(8,128)S(1)} %add.116), channel_id=1, source_target_pairs={{0,4},{4,0},{1,5},{5,1},{2,6},{6,2},{3,7},{7,3},{8,12},{12,8},{9,1... | collective-permute-start | bytes 1572872 | tf_op jit(solution)/shard_map/ppermute | solution.py:19
  46.1 8.3 %collective-permute-start.3 = (bf16[8,128,128]{2,1,0:T(8,128)(2,1)S(1)}, bf16[8,128,128]{2,1,0:T(8,128)(2,1)S(1)}, u32[]{:S(2)}, u32[]{:S(2)}) collective-permute-start(bf16[8,128,128]{2,1,0:T(8,128)(2,1)S(1)} %add_convert_fusion), channel_id=1, source_target_pairs={{0,8},{8,0},{16,24},{24,16},{1,9},{9,1},{17,25},{25,17},{2,10},{10... | collective-permute-start | bytes 786440 | tf_op jit(solution)/shard_map/ppermute | solution.py:19
  48.2 13.8 %copy-start.1 = (f32[8,512,128]{1,2,0:T(8,128)S(1)}, f32[8,512,128]{1,2,0:T(8,128)}, u32[]{:S(2)}) copy-start(f32[8,512,128]{1,2,0:T(8,128)} %fusion) | copy-start | bytes 6291460
  54.5 7.4 %collective-permute-start.4 = (bf16[8,128,128]{2,1,0:T(8,128)(2,1)S(1)}, bf16[8,128,128]{2,1,0:T(8,128)(2,1)S(1)}, u32[]{:S(2)}, u32[]{:S(2)}) collective-permute-start(bf16[8,128,128]{2,1,0:T(8,128)(2,1)S(1)} %fusion.38), channel_id=1, source_target_pairs={{0,16},{16,0},{8,24},{24,8},{1,17},{17,1},{9,25},{25,9},{2,18},{18... | collective-permute-start | bytes 786440 | tf_op jit(solution)/shard_map/ppermute | solution.py:19
where the time goes:
time: 64.5 us; the launch traced here: 64.3 us
  waiting for transfers between devices  41.5 us (64%)
  matrix products  12.6 us (20%)
  starting transfers between devices  4.13 us (6%)
  other arithmetic  3 us (5%)
  local copies, waits for them, and re-layouts  2.92 us (5%)
    ppermute x5, waiting for transfers between devices, from_partner(): return lax.ppermute(block, axis, route)  41.5 us
    dot_general x1, matrix products, local_part(): jnp.einsum('hts,shv->thv', weighted, value_matrix, preferred_element_type...  7.95 us
    ppermute x5, starting transfers between devices, from_partner(): return lax.ppermute(block, axis, route)  4.13 us
    dot_general x5, matrix products, on_device(): jnp.einsum('ryl,ylf->ryf', query_matrix, siblings[bit_num].astype(jnp.bfl...  2.94 us
    and x1, other arithmetic, local_part(): picked = jnp.logical_and(level_ids == level_num, causal)  1.7 us
    dot_general x1, matrix products, on_device(): jnp.einsum('pdx,pdo->dxo', key_matrix, value_matrix, preferred_element_ty...  1.68 us
    reshape x1, local copies, waits for them, and re-layouts, on_device(): key_matrix = keys.reshape(row_count, head_count, head_width)  1.59 us
    convert_element_type x1, local copies, waits for them, and re-layouts, on_device(): attended.reshape(row_count, head_count * head_width).astype(jnp.bfloat16)  1.32 us
  transfers between devices with their start and end apart: 5, of which 5 were waited for; matrix products, arithmetic and copies ran while one was open for 18% of the time, Pallas kernels for 0%

commit v1 on v0

v1 whole, which is shorter than its diff:
```python
import functools
import math

import jax
import jax.numpy as jnp
from jax import lax
from jax.experimental import pallas as pl
from jax.experimental.pallas import tpu as pltpu
from jax.sharding import PartitionSpec as P

DK = 128
STRETCH = 64
SUB = 2 * STRETCH
MESH = pl.DeviceIdType.MESH
LAG = 2


def level_factor(level_num):
    token_count = STRETCH if level_num == 0 else STRETCH * 2 ** (level_num - 1)
    return 1.0 / math.sqrt(DK * token_count)


def dot_nt(a, b):
    return lax.dot_general(a, b, (((1,), (1,)), ((), ())), preferred_element_type=jnp.float32)


def dot_nn(a, b):
    return lax.dot_general(a, b, (((1,), (0,)), ((), ())), preferred_element_type=jnp.float32)


def kernel(
    ctx_bits, grp_bits,
    q_hbm, k_hbm, v_hbm, w_hbm, out_hbm,
    q_buf, k_buf, v_buf, w_buf, w_head, vt_buf, sub_buf, state, sib, run, acc, out_t, out_buf,
    in_sem, w_sem, out_sem, send_sem, fwd_sem, recv_sem,
):
    heads, rows = q_buf.shape[0], q_buf.shape[1]
    half = heads // 2
    count = rows // SUB
    local_bits = (rows // STRETCH).bit_length() - 1
    depth = ctx_bits + grp_bits
    last = depth - 1
    grp = lax.axis_index("grp")
    ctx = lax.axis_index("ctx")
    core = ctx % 2

    def bit(j):
        if j < ctx_bits:
            return (ctx // 2**j) % 2
        return (grp // 2 ** (j - ctx_bits)) % 2

    def partner(j):
        step = 1 - 2 * bit(j)
        if j < ctx_bits:
            return (grp, ctx + step * 2**j)
        return (grp + step * 2 ** (j - ctx_bits), ctx)

    def mine(i):
        return core * half + i

    def other(i):
        return (1 - core) * half + i

    def columns(h):
        return pl.ds(pl.multiple_of(h * DK, DK), DK)

    def fetch(n, h):
        src, dst = ((q_hbm, q_buf), (k_hbm, k_buf), (v_hbm, v_buf))[n]
        return pltpu.make_async_copy(src.at[:, columns(h)], dst.at[h], in_sem.at[n, h])

    def fetch_w():
        return pltpu.make_async_copy(w_hbm, w_buf, w_sem)

    def put(h):
        return pltpu.make_async_copy(out_buf.at[h], out_hbm.at[:, columns(h)], out_sem.at[h])

    def remote(src, j, h, sem, target):
        return pltpu.make_async_remote_copy(
            src_ref=src, dst_ref=sib.at[j, h], send_sem=sem, recv_sem=recv_sem.at[j, h],
            device_id=target, device_id_type=MESH,
        )

    def first_send(h):
        return remote(state.at[h], 0, h, send_sem.at[0, h], partner(0))

    def stage_send(j, i):
        return remote(run.at[j, i], j, mine(i), send_sem.at[j, mine(i)], partner(j))

    def forward(j, i):
        h = mine(i)
        return remote(sib.at[j, h], j, h, fwd_sem.at[j, h], partner(0))

    def arrival(j, h):
        return remote(sib.at[j, h], j, h, send_sem.at[j, h], partner(0))

    def scale(level, h, start, size):
        return w_head[h, level : level + 1, start : start + size]

    barrier = pltpu.get_barrier_semaphore()
    for j in range(depth):
        pl.semaphore_signal(barrier, inc=1, device_id=partner(j), device_id_type=MESH)
    for i in range(half):
        for h in (other(i), mine(i)):
            fetch(1, h).start()
            fetch(2, h).start()
    fetch_w().start()
    for i in range(half):
        for h in (mine(i), other(i)):
            fetch(0, h).start()
    pl.semaphore_wait(barrier, depth)

    def block_sum(h):
        fetch(1, h).wait()
        fetch(2, h).wait()
        vt = v_buf[h].T
        vt_buf[h] = vt
        sums = [
            dot_nn(vt[:, b * SUB : (b + 1) * SUB], k_buf[h, b * SUB : (b + 1) * SUB, :])
            for b in range(count)
        ]
        slot = 0
        while len(sums) > 1:
            for b in range(0, len(sums), 2):
                sub_buf[h, slot] = sums[b].astype(jnp.bfloat16)
                slot += 1
            sums = [sums[b] + sums[b + 1] for b in range(0, len(sums), 2)]
        state[h] = sums[0].astype(jnp.bfloat16)
        first_send(h).start()

    def open_pair(i, carry):
        block_sum(other(i))
        block_sum(mine(i))
        return carry

    lax.fori_loop(0, half, open_pair, 0)
    fetch_w().wait()
    for level in range(1 + local_bits + depth):
        for h in range(heads):
            w_head[h, level : level + 1, :] = w_buf[level, h : h + 1, :] * level_factor(level)

    def local(h):
        fetch(0, h).wait()
        s = lax.broadcasted_iota(jnp.int32, (SUB, SUB), 0)
        t = lax.broadcasted_iota(jnp.int32, (SUB, SUB), 1)
        causal = s <= t
        crossing = jnp.logical_and(s < STRETCH, t >= STRETCH)
        for b in range(count):
            lo = b * SUB
            q = q_buf[h, lo : lo + SUB, :]
            scores = dot_nt(k_buf[h, lo : lo + SUB, :], q)
            weight = jnp.where(
                crossing, scale(1, h, lo, SUB), scale(0, h, lo, SUB)
            )
            weighted = jnp.where(causal, scores * weight, 0.0).astype(jnp.bfloat16)
            total = dot_nn(vt_buf[h, :, lo : lo + SUB], weighted)
            slot = 0
            for level in range(2, local_bits + 1):
                place = b >> (level - 2)
                if place % 2 == 1:
                    total += scale(level, h, lo, SUB) * dot_nt(sub_buf[h, slot + place // 2], q)
                slot += count >> (level - 1)
            out_t[h, :, lo : lo + SUB] = total

    def cross(j, h):
        level = 1 + local_bits + j
        out_t[h] += scale(level, h, 0, rows) * dot_nt(sib[j, h], q_buf[h])

    def finish(h):
        out_buf[h] = out_t[h].astype(jnp.bfloat16).T
        put(h).start()

    def receive(j, i):
        h = mine(i)
        if j == last:
            @pl.when(bit(j) == 1)
            def _():
                arrival(j, h).wait_recv()
        else:
            arrival(j, h).wait_recv()
        if j >= 1:
            @pl.when(bit(j) == 1)
            def _():
                forward(j, i).start()
        if j < last:
            held = state[h].astype(jnp.float32) if j == 0 else acc[i]
            total = held + sib[j, h].astype(jnp.float32)
            rounded = total.astype(jnp.bfloat16)
            run[j + 1, i] = rounded
            acc[i] = rounded.astype(jnp.float32) if j + 1 == ctx_bits else total
            if j + 1 == last:
                @pl.when(bit(j + 1) == 0)
                def _():
                    stage_send(j + 1, i).start()
            else:
                stage_send(j + 1, i).start()

    def wave(w, carry):
        for j in reversed(range(depth)):
            i = w - LAG * j

            @pl.when(jnp.logical_and(i >= 0, i < half))
            def _():
                receive(j, i)

        @pl.when(w < half)
        def _():
            local(mine(w))
            local(other(w))

        for j in range(depth):
            i = w - LAG * j

            @pl.when(jnp.logical_and(jnp.logical_and(i >= 0, i < half), bit(j) == 1))
            def _():
                cross(j, mine(i))

            @pl.when(jnp.logical_and(i >= 1, i < half + 1))
            def _():
                h = other(i - 1)
                if j == 0:
                    arrival(j, h).wait_recv()

                @pl.when(bit(j) == 1)
                def _():
                    if j > 0:
                        arrival(j, h).wait_recv()
                    cross(j, h)

        final = w - LAG * last

        @pl.when(jnp.logical_and(final >= 0, final < half))
        def _():
            finish(mine(final))

        @pl.when(final >= 1)
        def _():
            finish(other(final - 1))

        return carry

    lax.fori_loop(0, LAG * last + half + 1, wave, 0)

    def close(i, carry):
        for h in (mine(i), other(i)):
            first_send(h).wait_send()
            put(h).wait()
        for j in range(1, depth):
            if j == last:
                @pl.when(bit(j) == 0)
                def _():
                    stage_send(j, i).wait_send()
            else:
                stage_send(j, i).wait_send()

            @pl.when(bit(j) == 1)
            def _():
                forward(j, i).wait_send()
        return carry

    lax.fori_loop(0, half, close, 0)


def on_device(ctx_count, grp_count, queries, keys, values, level_weights):
    rows = queries.shape[0]
    heads = level_weights.shape[1]
    count = rows // SUB
    ctx_bits = ctx_count.bit_length() - 1
    grp_bits = grp_count.bit_length() - 1
    depth = ctx_bits + grp_bits
    half = heads // 2
    bf16, f32 = jnp.bfloat16, jnp.float32
    any_spec = pl.BlockSpec(memory_space=pl.ANY)
    return pl.pallas_call(
        functools.partial(kernel, ctx_bits, grp_bits),
        out_shape=jax.ShapeDtypeStruct(queries.shape, bf16),
        in_specs=[any_spec] * 4,
        out_specs=any_spec,
        scratch_shapes=[
            pltpu.VMEM((heads, rows, DK), bf16),
            pltpu.VMEM((heads, rows, DK), bf16),
            pltpu.VMEM((heads, rows, DK), bf16),
            pltpu.VMEM(level_weights.shape, f32),
            pltpu.VMEM((heads, level_weights.shape[0], rows), f32),
            pltpu.VMEM((heads, DK, rows), bf16),
            pltpu.VMEM((heads, count - 1, DK, DK), bf16),
            pltpu.VMEM((heads, DK, DK), bf16),
            pltpu.VMEM((depth, heads, DK, DK), bf16),
            pltpu.VMEM((depth, half, DK, DK), bf16),
            pltpu.VMEM((half, DK, DK), f32),
            pltpu.VMEM((heads, DK, rows), f32),
            pltpu.VMEM((heads, rows, DK), bf16),
            pltpu.SemaphoreType.DMA((3, heads)),
            pltpu.SemaphoreType.DMA,
            pltpu.SemaphoreType.DMA((heads,)),
            pltpu.SemaphoreType.DMA((depth, heads)),
            pltpu.SemaphoreType.DMA((depth, heads)),
            pltpu.SemaphoreType.DMA((depth, heads)),
        ],
        compiler_params=pltpu.CompilerParams(
            collective_id=0, has_side_effects=True, vmem_limit_bytes=40 * 2**20
        ),
        cost_estimate=pl.CostEstimate(
            flops=2 * rows * heads * DK * DK * (9 + depth), bytes_accessed=8 * rows * heads * DK,
            transcendentals=0,
        ),
    )(queries, keys, values, level_weights)


def solution(mesh):
    return jax.shard_map(
        functools.partial(on_device, mesh.shape["ctx"], mesh.shape["grp"]),
        mesh=mesh,
        in_specs=(
            P(("grp", "ctx"), None),
            P(("grp", "ctx"), None),
            P(("grp", "ctx"), None),
            P(None, None, ("grp", "ctx")),
        ),
        out_specs=P(("grp", "ctx"), None),
        check_vma=False,
    )
```

time: 64.5 us -> 31.7 us (0.49)
  the two profiles are of different devices: /device:TPU:24 before, /device:TPU:5 now
where the time goes in v1:
time: 31.7 us; the launch traced here: 31.5 us
  Pallas kernels  25.9 us (82%)
  local copies, waits for them, and re-layouts  5.58 us (18%)
    pallas_call x1, Pallas kernels, on_device(): pl.pallas_call(functools.partial(kernel, ctx_bits, grp_bits), out_shape=j...  25.9 us
    unnamed x9, local copies, waits for them, and re-layouts  5.58 us

profile of v1, /device:TPU:5, one launch (start us, length us, event | category | flops | bytes accessed | tf_op | source)
XLA Modules:
  0.0 31.5 jit_solution(9388405075277649739)
XLA Ops:
  0.0 0.0 copy-start
  0.0 1.2 %copy-done = bf16[512,1024]{1,0:T(8,128)(2,1)S(1)} copy-done((bf16[512,1024]{1,0:T(8,128)(2,1)S(1)}, bf16[512,1024]{1,0:T(8,128)(2,1)}, u32[]{:S(2)}) %copy-start) | copy-done | bytes 1048600
  1.2 0.0 copy-start.1
  1.2 1.2 %copy-done.1 = bf16[512,1024]{1,0:T(8,128)(2,1)S(1)} copy-done((bf16[512,1024]{1,0:T(8,128)(2,1)S(1)}, bf16[512,1024]{1,0:T(8,128)(2,1)}, u32[]{:S(2)}) %copy-start.1) | copy-done | bytes 1048600
  2.5 0.0 copy-start.2
  2.5 1.2 %copy-done.2 = bf16[512,1024]{1,0:T(8,128)(2,1)S(1)} copy-done((bf16[512,1024]{1,0:T(8,128)(2,1)S(1)}, bf16[512,1024]{1,0:T(8,128)(2,1)}, u32[]{:S(2)}) %copy-start.2) | copy-done | bytes 1048600
  3.7 0.0 copy-start.3
  3.7 0.9 %copy-done.3 = f32[13,8,512]{2,1,0:T(8,128)S(1)} copy-done((f32[13,8,512]{2,1,0:T(8,128)S(1)}, f32[13,8,512]{2,1,0:T(8,128)}, u32[]{:S(2)}) %copy-start.3) | copy-done | bytes 213016
  4.6 25.9 %shard_map.46 = bf16[512,1024]{1,0:T(8,128)(2,1)S(1)} custom-call(bf16[512,1024]{1,0:T(8,128)(2,1)S(1)} %copy-done, bf16[512,1024]{1,0:T(8,128)(2,1)S(1)} %copy-done.1, bf16[512,1024]{1,0:T(8,128)(2,1)S(1)} %copy-done.2, f32[13,8,512]{2,1,0:T(8,128)S(1)} %copy-done.3), custom_call_target="tpu_custom_call" | custom-call | flops 1879048192 | bytes 4194304 | tf_op jit(solution)/shard_map/pallas_call | solution.py:273
  30.5 1.0 %copy.6 = bf16[512,1024]{1,0:T(8,128)(2,1)} copy(bf16[512,1024]{1,0:T(8,128)(2,1)S(1)} %shard_map.46) | data formatting | bytes 2097152
Async XLA Ops:
  0.0 1.2 %copy-start = (bf16[512,1024]{1,0:T(8,128)(2,1)S(1)}, bf16[512,1024]{1,0:T(8,128)(2,1)}, u32[]{:S(2)}) copy-start(bf16[512,1024]{1,0:T(8,128)(2,1)} %q_hbm.1) | copy-start | bytes 3145732
  1.2 1.2 %copy-start.1 = (bf16[512,1024]{1,0:T(8,128)(2,1)S(1)}, bf16[512,1024]{1,0:T(8,128)(2,1)}, u32[]{:S(2)}) copy-start(bf16[512,1024]{1,0:T(8,128)(2,1)} %k_hbm.1) | copy-start | bytes 3145732
  2.5 1.2 %copy-start.2 = (bf16[512,1024]{1,0:T(8,128)(2,1)S(1)}, bf16[512,1024]{1,0:T(8,128)(2,1)}, u32[]{:S(2)}) copy-start(bf16[512,1024]{1,0:T(8,128)(2,1)} %v_hbm.1) | copy-start | bytes 3145732
  3.7 0.9 %copy-start.3 = (f32[13,8,512]{2,1,0:T(8,128)S(1)}, f32[13,8,512]{2,1,0:T(8,128)}, u32[]{:S(2)}) copy-start(f32[13,8,512]{2,1,0:T(8,128)} %w_hbm.1) | copy-start | bytes 638980

commit v2 on v1

--- a/solution.py
+++ b/solution.py
@@ -11,8 +11,8 @@
 DK = 128
 STRETCH = 64
 SUB = 2 * STRETCH
+RELAYED = 2
 MESH = pl.DeviceIdType.MESH
-LAG = 2
 
 
 def level_factor(level_num):
@@ -32,7 +32,7 @@
     ctx_bits, grp_bits,
     q_hbm, k_hbm, v_hbm, w_hbm, out_hbm,
     q_buf, k_buf, v_buf, w_buf, w_head, vt_buf, sub_buf, state, sib, run, acc, out_t, out_buf,
-    in_sem, w_sem, out_sem, send_sem, fwd_sem, recv_sem,
+    in_sem, w_sem, out_sem, send_sem, fwd_sem, relay_sem, recv_sem,
 ):
     heads, rows = q_buf.shape[0], q_buf.shape[1]
     half = heads // 2
@@ -49,8 +49,12 @@
             return (ctx // 2**j) % 2
         return (grp // 2 ** (j - ctx_bits)) % 2
 
+    inner = (bit(1) + bit(2)) % 2
+
     def partner(j):
         step = 1 - 2 * bit(j)
+        if j == RELAYED:
+            return (grp, ctx + step * 2)
         if j < ctx_bits:
             return (grp, ctx + step * 2**j)
         return (grp + step * 2 ** (j - ctx_bits), ctx)
@@ -90,6 +94,10 @@
         h = mine(i)
         return remote(sib.at[j, h], j, h, fwd_sem.at[j, h], partner(0))
 
+    def relay(i):
+        h = mine(i)
+        return remote(sib.at[RELAYED, h], RELAYED, h, relay_sem.at[h], partner(1))
+
     def arrival(j, h):
         return remote(sib.at[j, h], j, h, send_sem.at[j, h], partner(0))
 
@@ -97,17 +105,24 @@
         return w_head[h, level : level + 1, start : start + size]
 
     barrier = pltpu.get_barrier_semaphore()
-    for j in range(depth):
-        pl.semaphore_signal(barrier, inc=1, device_id=partner(j), device_id_type=MESH)
     for i in range(half):
         for h in (other(i), mine(i)):
             fetch(1, h).start()
             fetch(2, h).start()
+        if i == 0:
+            for j in range(depth):
+                if j == RELAYED:
+                    @pl.when(inner == 1)
+                    def _():
+                        pl.semaphore_signal(
+                            barrier, inc=1, device_id=partner(j), device_id_type=MESH
+                        )
+                else:
+                    pl.semaphore_signal(barrier, inc=1, device_id=partner(j), device_id_type=MESH)
     fetch_w().start()
     for i in range(half):
         for h in (mine(i), other(i)):
             fetch(0, h).start()
-    pl.semaphore_wait(barrier, depth)
 
     def block_sum(h):
         fetch(1, h).wait()
@@ -125,18 +140,13 @@
                 slot += 1
             sums = [sums[b] + sums[b + 1] for b in range(0, len(sums), 2)]
         state[h] = sums[0].astype(jnp.bfloat16)
-        first_send(h).start()
-
-    def open_pair(i, carry):
-        block_sum(other(i))
-        block_sum(mine(i))
-        return carry
-
-    lax.fori_loop(0, half, open_pair, 0)
-    fetch_w().wait()
-    for level in range(1 + local_bits + depth):
-        for h in range(heads):
-            w_head[h, level : level + 1, :] = w_buf[level, h : h + 1, :] * level_factor(level)
+
+    def first_sends(i):
+        first_send(other(i)).start()
+
+        @pl.when(core == 0)
+        def _():
+            first_send(mine(i)).start()
 
     def local(h):
         fetch(0, h).wait()
@@ -169,34 +179,56 @@
         out_buf[h] = out_t[h].astype(jnp.bfloat16).T
         put(h).start()
 
+    def guarded(condition, action):
+        if condition is None:
+            action()
+        else:
+            pl.when(condition)(action)
+
+    def sends(j):
+        if j == RELAYED:
+            return inner == 1
+        return bit(j) == 0 if j == last else None
+
     def receive(j, i):
         h = mine(i)
-        if j == last:
-            @pl.when(bit(j) == 1)
-            def _():
-                arrival(j, h).wait_recv()
-        else:
-            arrival(j, h).wait_recv()
+        guarded(bit(j) == 1 if j == last else None, lambda: arrival(j, h).wait_recv())
+        if j == RELAYED:
+            guarded(inner == 1, lambda: relay(i).start())
         if j >= 1:
-            @pl.when(bit(j) == 1)
-            def _():
-                forward(j, i).start()
+            guarded(bit(j) == 1, lambda: forward(j, i).start())
         if j < last:
             held = state[h].astype(jnp.float32) if j == 0 else acc[i]
             total = held + sib[j, h].astype(jnp.float32)
             rounded = total.astype(jnp.bfloat16)
             run[j + 1, i] = rounded
             acc[i] = rounded.astype(jnp.float32) if j + 1 == ctx_bits else total
-            if j + 1 == last:
-                @pl.when(bit(j + 1) == 0)
-                def _():
-                    stage_send(j + 1, i).start()
-            else:
-                stage_send(j + 1, i).start()
+            guarded(sends(j + 1), lambda: stage_send(j + 1, i).start())
+
+    block_sum(other(0))
+    block_sum(mine(0))
+    pl.semaphore_wait(barrier, depth - 1 + inner)
+    first_sends(0)
+
+    def open_pair(i, carry):
+        block_sum(other(i))
+        block_sum(mine(i))
+        first_sends(i)
+        receive(0, i - 1)
+        return carry
+
+    lax.fori_loop(1, half, open_pair, 0)
+    receive(0, half - 1)
+    fetch_w().wait()
+    for level in range(1 + local_bits + depth):
+        for h in range(heads):
+            w_head[h, level : level + 1, :] = w_buf[level, h : h + 1, :] * level_factor(level)
+
+    lag = [0, 1] + [half + 2 * j for j in range(depth - 2)]
 
     def wave(w, carry):
-        for j in reversed(range(depth)):
-            i = w - LAG * j
+        for j in range(1, depth):
+            i = w - lag[j]
 
             @pl.when(jnp.logical_and(i >= 0, i < half))
             def _():
@@ -208,25 +240,20 @@
             local(other(w))
 
         for j in range(depth):
-            i = w - LAG * j
-
-            @pl.when(jnp.logical_and(jnp.logical_and(i >= 0, i < half), bit(j) == 1))
+            i = w - lag[j]
+            held = bit(j) == 1
+
+            @pl.when(jnp.logical_and(jnp.logical_and(i >= 0, i < half), held))
             def _():
                 cross(j, mine(i))
 
-            @pl.when(jnp.logical_and(i >= 1, i < half + 1))
+            @pl.when(jnp.logical_and(jnp.logical_and(i >= 1, i < half + 1), held))
             def _():
                 h = other(i - 1)
-                if j == 0:
-                    arrival(j, h).wait_recv()
-
-                @pl.when(bit(j) == 1)
-                def _():
-                    if j > 0:
-                        arrival(j, h).wait_recv()
-                    cross(j, h)
-
-        final = w - LAG * last
+                arrival(j, h).wait_recv()
+                cross(j, h)
+
+        final = w - lag[last]
 
         @pl.when(jnp.logical_and(final >= 0, final < half))
         def _():
@@ -238,23 +265,18 @@
 
         return carry
 
-    lax.fori_loop(0, LAG * last + half + 1, wave, 0)
+    lax.fori_loop(0, lag[last] + half + 1, wave, 0)
 
     def close(i, carry):
+        first_send(other(i)).wait_send()
+        guarded(core == 0, lambda: first_send(mine(i)).wait_send())
         for h in (mine(i), other(i)):
-            first_send(h).wait_send()
             put(h).wait()
         for j in range(1, depth):
-            if j == last:
-                @pl.when(bit(j) == 0)
-                def _():
-                    stage_send(j, i).wait_send()
-            else:
-                stage_send(j, i).wait_send()
-
-            @pl.when(bit(j) == 1)
-            def _():
-                forward(j, i).wait_send()
+            guarded(sends(j), lambda: stage_send(j, i).wait_send())
+            guarded(bit(j) == 1, lambda: forward(j, i).wait_send())
+            if j == RELAYED:
+                guarded(inner == 1, lambda: relay(i).wait_send())
         return carry
 
     lax.fori_loop(0, half, close, 0)
@@ -273,7 +295,7 @@
     return pl.pallas_call(
         functools.partial(kernel, ctx_bits, grp_bits),
         out_shape=jax.ShapeDtypeStruct(queries.shape, bf16),
-        in_specs=[any_spec] * 4,
+        in_specs=[pl.BlockSpec(memory_space=pltpu.HBM)] * 4,
         out_specs=any_spec,
         scratch_shapes=[
             pltpu.VMEM((heads, rows, DK), bf16),
@@ -294,10 +316,11 @@
             pltpu.SemaphoreType.DMA((heads,)),
             pltpu.SemaphoreType.DMA((depth, heads)),
             pltpu.SemaphoreType.DMA((depth, heads)),
+            pltpu.SemaphoreType.DMA((heads,)),
             pltpu.SemaphoreType.DMA((depth, heads)),
         ],
         compiler_params=pltpu.CompilerParams(
-            collective_id=0, has_side_effects=True, vmem_limit_bytes=40 * 2**20
+            collective_id=0, has_side_effects=True, vmem_limit_bytes=60 * 2**20
         ),
         cost_estimate=pl.CostEstimate(
             flops=2 * rows * heads * DK * DK * (9 + depth), bytes_accessed=8 * rows * heads * DK,

time: 31.7 us -> 29.8 us (0.940)
  local copies, waits for them, and re-layouts: 5.58 us -> 2.26 us
  Pallas kernels: 25.9 us -> 27.4 us
    unnamed x9 -> x1, local copies, waits for them, and re-layouts: 5.58 us -> 2.26 us
    pallas_call x1, Pallas kernels: 25.9 us -> 27.4 us  [on_device(): pl.pallas_call(functools.partial(kernel, ctx_bits, grp_bits), out_shape=j...]
where the time goes in v2:
time: 29.8 us; the launch traced here: 29.7 us
  Pallas kernels  27.4 us (92%)
  local copies, waits for them, and re-layouts  2.26 us (8%)
    pallas_call x1, Pallas kernels, on_device(): pl.pallas_call(functools.partial(kernel, ctx_bits, grp_bits), out_shape=j...  27.4 us
    unnamed x1, local copies, waits for them, and re-layouts  2.26 us

profile of v2, /device:TPU:5, one launch (start us, length us, event | category | flops | bytes accessed | tf_op | source)
XLA Modules:
  0.0 29.7 jit_solution(4803878933602962297)
XLA Ops:
  0.0 27.4 %shard_map.46 = bf16[512,1024]{1,0:T(8,128)(2,1)} custom-call(bf16[512,1024]{1,0:T(8,128)(2,1)} %q_hbm.1, bf16[512,1024]{1,0:T(8,128)(2,1)} %k_hbm.1, bf16[512,1024]{1,0:T(8,128)(2,1)} %v_hbm.1, f32[13,8,512]{2,1,0:T(8,128)} %w_hbm.1), custom_call_target="tpu_custom_call" | custom-call | flops 1879048192 | bytes 4194304 | tf_op jit(solution)/shard_map/pallas_call | solution.py:295
  27.4 2.3 %copy.6 = bf16[512,1024]{1,0:T(8,128)(2,1)} copy(bf16[512,1024]{1,0:T(8,128)(2,1)} %shard_map.46) | data formatting | bytes 2097152

commit v3 on v2

--- a/solution.py
+++ b/solution.py
@@ -31,7 +31,7 @@
 def kernel(
     ctx_bits, grp_bits,
     q_hbm, k_hbm, v_hbm, w_hbm, out_hbm,
-    q_buf, k_buf, v_buf, w_buf, w_head, vt_buf, sub_buf, state, sib, run, acc, out_t, out_buf,
+    q_buf, k_buf, v_buf, w_buf, w_head, vt_buf, qt_buf, sub_buf, state, sib, run, acc, out_t, out_buf,
     in_sem, w_sem, out_sem, send_sem, fwd_sem, relay_sem, recv_sem,
 ):
     heads, rows = q_buf.shape[0], q_buf.shape[1]
@@ -76,7 +76,7 @@
         return pltpu.make_async_copy(w_hbm, w_buf, w_sem)
 
     def put(h):
-        return pltpu.make_async_copy(out_buf.at[h], out_hbm.at[:, columns(h)], out_sem.at[h])
+        return pltpu.make_async_copy(out_buf.at[h], out_hbm.at[h], out_sem.at[h])
 
     def remote(src, j, h, sem, target):
         return pltpu.make_async_remote_copy(
@@ -148,35 +148,58 @@
         def _():
             first_send(mine(i)).start()
 
+    def scaled(level, h, qt, lo, size):
+        return (scale(level, h, lo, size) * qt).astype(jnp.bfloat16)
+
+    def sibling(j, h):
+        return jnp.where(bit(j) == 1, sib[j, h], jnp.zeros((DK, DK), jnp.bfloat16))
+
     def local(h):
         fetch(0, h).wait()
+        qt_all = q_buf[h].T
+        qt_buf[h] = qt_all
         s = lax.broadcasted_iota(jnp.int32, (SUB, SUB), 0)
         t = lax.broadcasted_iota(jnp.int32, (SUB, SUB), 1)
         causal = s <= t
         crossing = jnp.logical_and(s < STRETCH, t >= STRETCH)
+        neighbour = sibling(0, h)
         for b in range(count):
             lo = b * SUB
-            q = q_buf[h, lo : lo + SUB, :]
-            scores = dot_nt(k_buf[h, lo : lo + SUB, :], q)
+            qt = qt_all[:, lo : lo + SUB]
+            scores = dot_nn(k_buf[h, lo : lo + SUB, :], qt)
             weight = jnp.where(
                 crossing, scale(1, h, lo, SUB), scale(0, h, lo, SUB)
             )
             weighted = jnp.where(causal, scores * weight, 0.0).astype(jnp.bfloat16)
-            total = dot_nn(vt_buf[h, :, lo : lo + SUB], weighted)
+            wide = qt.astype(jnp.float32)
+            left = [vt_buf[h, :, lo : lo + SUB], neighbour]
+            right = [weighted, scaled(1 + local_bits, h, wide, lo, SUB)]
             slot = 0
             for level in range(2, local_bits + 1):
                 place = b >> (level - 2)
                 if place % 2 == 1:
-                    total += scale(level, h, lo, SUB) * dot_nt(sub_buf[h, slot + place // 2], q)
+                    left.append(sub_buf[h, slot + place // 2])
+                    right.append(scaled(level, h, wide, lo, SUB))
                 slot += count >> (level - 1)
-            out_t[h, :, lo : lo + SUB] = total
-
-    def cross(j, h):
-        level = 1 + local_bits + j
-        out_t[h] += scale(level, h, 0, rows) * dot_nt(sib[j, h], q_buf[h])
+            out_t[h, :, lo : lo + SUB] = dot_nn(
+                jnp.concatenate(left, axis=1), jnp.concatenate(right, axis=0)
+            )
+
+    def cross(group, h):
+        wide = qt_buf[h].astype(jnp.float32)
+        left = [sibling(j, h) for j in group]
+        right = [scaled(1 + local_bits + j, h, wide, 0, rows) for j in group]
+        return out_t[h] + dot_nn(jnp.concatenate(left, axis=1), jnp.concatenate(right, axis=0))
+
+    def await_other(group, h):
+        for j in group:
+            guarded(bit(j) == 1, lambda: arrival(j, h).wait_recv())
+
+    def middle(h):
+        out_t[h] = cross(range(1, ctx_bits), h)
 
     def finish(h):
-        out_buf[h] = out_t[h].astype(jnp.bfloat16).T
+        out_buf[h] = cross(range(ctx_bits, depth), h).astype(jnp.bfloat16)
         put(h).start()
 
     def guarded(condition, action):
@@ -224,43 +247,44 @@
         for h in range(heads):
             w_head[h, level : level + 1, :] = w_buf[level, h : h + 1, :] * level_factor(level)
 
-    lag = [0, 1] + [half + 2 * j for j in range(depth - 2)]
+    lag = [0, 1, half] + [2 * half + 2 * j for j in range(depth - 3)]
+    lag_middle = max(2 * half, lag[ctx_bits - 1] + 1)
+
+    def between(i, low, high):
+        return jnp.logical_and(i >= low, i < high)
 
     def wave(w, carry):
         for j in range(1, depth):
             i = w - lag[j]
-
-            @pl.when(jnp.logical_and(i >= 0, i < half))
+            guarded(between(i, 0, half), functools.partial(receive, j, i))
+
+        @pl.when(w < heads)
+        def _():
+            h = ((core + w) % 2) * half + w // 2
+
+            @pl.when(jnp.logical_and(w % 2 == 1, bit(0) == 1))
             def _():
-                receive(j, i)
-
-        @pl.when(w < half)
-        def _():
-            local(mine(w))
-            local(other(w))
-
-        for j in range(depth):
-            i = w - lag[j]
-            held = bit(j) == 1
-
-            @pl.when(jnp.logical_and(jnp.logical_and(i >= 0, i < half), held))
-            def _():
-                cross(j, mine(i))
-
-            @pl.when(jnp.logical_and(jnp.logical_and(i >= 1, i < half + 1), held))
-            def _():
-                h = other(i - 1)
-                arrival(j, h).wait_recv()
-                cross(j, h)
+                arrival(0, h).wait_recv()
+
+            local(h)
+
+        i_middle = w - lag_middle
+
+        @pl.when(between(i_middle, 0, half))
+        def _():
+            middle(mine(i_middle))
+            await_other(range(1, ctx_bits), other(i_middle))
+            middle(other(i_middle))
 
         final = w - lag[last]
 
-        @pl.when(jnp.logical_and(final >= 0, final < half))
+        @pl.when(between(final, 0, half))
         def _():
             finish(mine(final))
 
         @pl.when(final >= 1)
         def _():
+            await_other(range(ctx_bits, depth), other(final - 1))
             finish(other(final - 1))
 
         return carry
@@ -292,9 +316,9 @@
     half = heads // 2
     bf16, f32 = jnp.bfloat16, jnp.float32
     any_spec = pl.BlockSpec(memory_space=pl.ANY)
-    return pl.pallas_call(
+    out = pl.pallas_call(
         functools.partial(kernel, ctx_bits, grp_bits),
-        out_shape=jax.ShapeDtypeStruct(queries.shape, bf16),
+        out_shape=jax.ShapeDtypeStruct((heads, DK, rows), bf16),
         in_specs=[pl.BlockSpec(memory_space=pltpu.HBM)] * 4,
         out_specs=any_spec,
         scratch_shapes=[
@@ -304,13 +328,14 @@
             pltpu.VMEM(level_weights.shape, f32),
             pltpu.VMEM((heads, level_weights.shape[0], rows), f32),
             pltpu.VMEM((heads, DK, rows), bf16),
+            pltpu.VMEM((heads, DK, rows), bf16),
             pltpu.VMEM((heads, count - 1, DK, DK), bf16),
             pltpu.VMEM((heads, DK, DK), bf16),
             pltpu.VMEM((depth, heads, DK, DK), bf16),
             pltpu.VMEM((depth, half, DK, DK), bf16),
             pltpu.VMEM((half, DK, DK), f32),
             pltpu.VMEM((heads, DK, rows), f32),
-            pltpu.VMEM((heads, rows, DK), bf16),
+            pltpu.VMEM((heads, DK, rows), bf16),
             pltpu.SemaphoreType.DMA((3, heads)),
             pltpu.SemaphoreType.DMA,
             pltpu.SemaphoreType.DMA((heads,)),
@@ -327,6 +352,7 @@
             transcendentals=0,
         ),
     )(queries, keys, values, level_weights)
+    return out.transpose(2, 0, 1).reshape(rows, heads * DK)
 
 
 def solution(mesh):

time: 29.8 us -> 27.1 us (0.909)
  Pallas kernels: 27.4 us -> 24.7 us
    pallas_call x1, Pallas kernels: 27.4 us -> 24.7 us  [on_device(): pl.pallas_call(functools.partial(kernel, ctx_bits, grp_bits), out_shape=j...]
    reshape x0 -> x1, local copies, waits for them, and re-layouts: none -> 2.27 us  [on_device(): return out.transpose(2, 0, 1).reshape(rows, heads * DK)]
    unnamed x1 -> x0, local copies, waits for them, and re-layouts: 2.26 us -> none
where the time goes in v3:
time: 27.1 us; the launch traced here: 27 us
  Pallas kernels  24.7 us (91%)
  local copies, waits for them, and re-layouts  2.27 us (8%)
    pallas_call x1, Pallas kernels, on_device(): pl.pallas_call(functools.partial(kernel, ctx_bits, grp_bits), out_shape=j...  24.7 us
    reshape x1, local copies, waits for them, and re-layouts, on_device(): return out.transpose(2, 0, 1).reshape(rows, heads * DK)  2.27 us

profile of v3, /device:TPU:5, one launch (start us, length us, event | category | flops | bytes accessed | tf_op | source)
XLA Modules:
  0.0 27.0 jit_solution(8503790958706532314)
XLA Ops:
  0.0 24.7 %shard_map.46 = bf16[8,128,512]{2,1,0:T(8,128)(2,1)} custom-call(bf16[512,1024]{1,0:T(8,128)(2,1)} %q_hbm.1, bf16[512,1024]{1,0:T(8,128)(2,1)} %k_hbm.1, bf16[512,1024]{1,0:T(8,128)(2,1)} %v_hbm.1, f32[13,8,512]{2,1,0:T(8,128)} %w_hbm.1), custom_call_target="tpu_custom_call" | custom-call | flops 1879048192 | bytes 4194304 | tf_op jit(solution)/shard_map/pallas_call | solution.py:319
  24.7 2.3 %copy.5 = bf16[512,1024]{1,0:T(8,128)(2,1)} copy(bf16[512,1024]{0,1:T(8,128)(2,1)} %bitcast.3) | data formatting | bytes 2097152 | tf_op jit(solution)/shard_map/reshape | solution.py:355

commit v4 on v3

--- a/solution.py
+++ b/solution.py
@@ -76,7 +76,7 @@
         return pltpu.make_async_copy(w_hbm, w_buf, w_sem)
 
     def put(h):
-        return pltpu.make_async_copy(out_buf.at[h], out_hbm.at[h], out_sem.at[h])
+        return pltpu.make_async_copy(out_buf.at[h], out_hbm.at[:, columns(h)], out_sem.at[h])
 
     def remote(src, j, h, sem, target):
         return pltpu.make_async_remote_copy(
@@ -199,7 +199,7 @@
         out_t[h] = cross(range(1, ctx_bits), h)
 
     def finish(h):
-        out_buf[h] = cross(range(ctx_bits, depth), h).astype(jnp.bfloat16)
+        out_buf[h] = cross(range(ctx_bits, depth), h).T
         put(h).start()
 
     def guarded(condition, action):
@@ -241,14 +241,15 @@
         return carry
 
     lax.fori_loop(1, half, open_pair, 0)
-    receive(0, half - 1)
     fetch_w().wait()
     for level in range(1 + local_bits + depth):
         for h in range(heads):
             w_head[h, level : level + 1, :] = w_buf[level, h : h + 1, :] * level_factor(level)
 
-    lag = [0, 1, half] + [2 * half + 2 * j for j in range(depth - 3)]
-    lag_middle = max(2 * half, lag[ctx_bits - 1] + 1)
+    receive(0, half - 1)
+
+    lag = [0] + [1 + 2 * j for j in range(depth - 1)]
+    lag_middle = max(half + 2, lag[ctx_bits - 1] + 1)
 
     def between(i, low, high):
         return jnp.logical_and(i >= low, i < high)
@@ -318,7 +319,7 @@
     any_spec = pl.BlockSpec(memory_space=pl.ANY)
     out = pl.pallas_call(
         functools.partial(kernel, ctx_bits, grp_bits),
-        out_shape=jax.ShapeDtypeStruct((heads, DK, rows), bf16),
+        out_shape=jax.ShapeDtypeStruct(queries.shape, f32),
         in_specs=[pl.BlockSpec(memory_space=pltpu.HBM)] * 4,
         out_specs=any_spec,
         scratch_shapes=[
@@ -335,7 +336,7 @@
             pltpu.VMEM((depth, half, DK, DK), bf16),
             pltpu.VMEM((half, DK, DK), f32),
             pltpu.VMEM((heads, DK, rows), f32),
-            pltpu.VMEM((heads, DK, rows), bf16),
+            pltpu.VMEM((heads, rows, DK), f32),
             pltpu.SemaphoreType.DMA((3, heads)),
             pltpu.SemaphoreType.DMA,
             pltpu.SemaphoreType.DMA((heads,)),
@@ -352,7 +353,7 @@
             transcendentals=0,
         ),
     )(queries, keys, values, level_weights)
-    return out.transpose(2, 0, 1).reshape(rows, heads * DK)
+    return out.astype(bf16)
 
 
 def solution(mesh):

time: 27.1 us -> 29.3 us (1.081)
  other arithmetic: 0 us -> 2.73 us
  local copies, waits for them, and re-layouts: 2.27 us -> 0 us
  Pallas kernels: 24.7 us -> 26.4 us
    convert_element_type x0 -> x1, other arithmetic: none -> 2.73 us  [on_device(): return out.astype(bf16)]
    reshape x1 -> x0, local copies, waits for them, and re-layouts: 2.27 us -> none  [on_device(): return out.transpose(2, 0, 1).reshape(rows, heads * DK)]
    pallas_call x1, Pallas kernels: 24.7 us -> 26.4 us  [on_device(): pl.pallas_call(functools.partial(kernel, ctx_bits, grp_bits), out_shape=j...]
where the time goes in v4:
time: 29.3 us; the launch traced here: 29.1 us
  Pallas kernels  26.4 us (90%)
  other arithmetic  2.73 us (9%)
    pallas_call x1, Pallas kernels, on_device(): pl.pallas_call(functools.partial(kernel, ctx_bits, grp_bits), out_shape=j...  26.4 us
    convert_element_type x1, other arithmetic, on_device(): return out.astype(bf16)  2.73 us

profile of v4, /device:TPU:5, one launch (start us, length us, event | category | flops | bytes accessed | tf_op | source)
XLA Modules:
  0.0 29.1 jit_solution(5545921005421254449)
XLA Ops:
  0.0 26.4 %shard_map.46 = f32[512,1024]{1,0:T(8,128)} custom-call(bf16[512,1024]{1,0:T(8,128)(2,1)} %q_hbm.1, bf16[512,1024]{1,0:T(8,128)(2,1)} %k_hbm.1, bf16[512,1024]{1,0:T(8,128)(2,1)} %v_hbm.1, f32[13,8,512]{2,1,0:T(8,128)} %w_hbm.1), custom_call_target="tpu_custom_call" | custom-call | flops 1879048192 | bytes 4194304 | tf_op jit(solution)/shard_map/pallas_call | solution.py:320
  26.4 2.7 %convert_element_type.3 = bf16[512,1024]{1,0:T(8,128)(2,1)} convert(f32[512,1024]{1,0:T(8,128)} %shard_map.46) | non-fusion elementwise | flops 524288 | bytes 3145728 | tf_op jit(solution)/shard_map/convert_element_type | solution.py:356

commit v5 on v3

--- a/solution.py
+++ b/solution.py
@@ -124,9 +124,14 @@
         for h in (mine(i), other(i)):
             fetch(0, h).start()
 
+    def block_sums(i):
+        for h in (other(i), mine(i)):
+            fetch(1, h).wait()
+            fetch(2, h).wait()
+        for h in (other(i), mine(i)):
+            block_sum(h)
+
     def block_sum(h):
-        fetch(1, h).wait()
-        fetch(2, h).wait()
         vt = v_buf[h].T
         vt_buf[h] = vt
         sums = [
@@ -155,7 +160,6 @@
         return jnp.where(bit(j) == 1, sib[j, h], jnp.zeros((DK, DK), jnp.bfloat16))
 
     def local(h):
-        fetch(0, h).wait()
         qt_all = q_buf[h].T
         qt_buf[h] = qt_all
         s = lax.broadcasted_iota(jnp.int32, (SUB, SUB), 0)
@@ -196,11 +200,10 @@
             guarded(bit(j) == 1, lambda: arrival(j, h).wait_recv())
 
     def middle(h):
-        out_t[h] = cross(range(1, ctx_bits), h)
+        return cross(range(1, ctx_bits), h)
 
     def finish(h):
-        out_buf[h] = cross(range(ctx_bits, depth), h).astype(jnp.bfloat16)
-        put(h).start()
+        return cross(range(ctx_bits, depth), h).astype(jnp.bfloat16)
 
     def guarded(condition, action):
         if condition is None:
@@ -228,27 +231,25 @@
             acc[i] = rounded.astype(jnp.float32) if j + 1 == ctx_bits else total
             guarded(sends(j + 1), lambda: stage_send(j + 1, i).start())
 
-    block_sum(other(0))
-    block_sum(mine(0))
+    block_sums(0)
     pl.semaphore_wait(barrier, depth - 1 + inner)
     first_sends(0)
 
     def open_pair(i, carry):
-        block_sum(other(i))
-        block_sum(mine(i))
+        block_sums(i)
         first_sends(i)
         receive(0, i - 1)
         return carry
 
     lax.fori_loop(1, half, open_pair, 0)
-    receive(0, half - 1)
     fetch_w().wait()
     for level in range(1 + local_bits + depth):
         for h in range(heads):
             w_head[h, level : level + 1, :] = w_buf[level, h : h + 1, :] * level_factor(level)
 
-    lag = [0, 1, half] + [2 * half + 2 * j for j in range(depth - 3)]
-    lag_middle = max(2 * half, lag[ctx_bits - 1] + 1)
+    receive(0, half - 1)
+    lag = [0] + [1 + 2 * j for j in range(depth - 1)]
+    lag_middle = max(half + 1, lag[ctx_bits - 1] + 1)
 
     def between(i, low, high):
         return jnp.logical_and(i >= low, i < high)
@@ -258,34 +259,46 @@
             i = w - lag[j]
             guarded(between(i, 0, half), functools.partial(receive, j, i))
 
-        @pl.when(w < heads)
-        def _():
-            h = ((core + w) % 2) * half + w // 2
-
-            @pl.when(jnp.logical_and(w % 2 == 1, bit(0) == 1))
-            def _():
-                arrival(0, h).wait_recv()
-
-            local(h)
+        @pl.when(w < half)
+        def _():
+            await_other(range(1), other(w))
+            for h in (mine(w), other(w)):
+                fetch(0, h).wait()
+            for h in (mine(w), other(w)):
+                local(h)
 
         i_middle = w - lag_middle
 
         @pl.when(between(i_middle, 0, half))
         def _():
-            middle(mine(i_middle))
             await_other(range(1, ctx_bits), other(i_middle))
-            middle(other(i_middle))
+            first = middle(mine(i_middle))
+            second = middle(other(i_middle))
+            out_t[mine(i_middle)] = first
+            out_t[other(i_middle)] = second
 
         final = w - lag[last]
 
-        @pl.when(between(final, 0, half))
-        def _():
-            finish(mine(final))
-
-        @pl.when(final >= 1)
+        @pl.when(between(final, 1, half))
         def _():
             await_other(range(ctx_bits, depth), other(final - 1))
-            finish(other(final - 1))
+            first = finish(mine(final))
+            second = finish(other(final - 1))
+            out_buf[mine(final)] = first
+            out_buf[other(final - 1)] = second
+            put(mine(final)).start()
+            put(other(final - 1)).start()
+
+        @pl.when(final == 0)
+        def _():
+            out_buf[mine(final)] = finish(mine(final))
+            put(mine(final)).start()
+
+        @pl.when(final == half)
+        def _():
+            await_other(range(ctx_bits, depth), other(final - 1))
+            out_buf[other(final - 1)] = finish(other(final - 1))
+            put(other(final - 1)).start()
 
         return carry
 

time: 27.1 us -> 27.7 us (1.022)
  Pallas kernels: 24.7 us -> 25.2 us
    pallas_call x1, Pallas kernels: 24.7 us -> 25.2 us  [on_device(): pl.pallas_call(functools.partial(kernel, ctx_bits, grp_bits), out_shape=j...]
where the time goes in v5:
time: 27.7 us; the launch traced here: 27.5 us
  Pallas kernels  25.2 us (91%)
  local copies, waits for them, and re-layouts  2.27 us (8%)
    pallas_call x1, Pallas kernels, on_device(): pl.pallas_call(functools.partial(kernel, ctx_bits, grp_bits), out_shape=j...  25.2 us
    reshape x1, local copies, waits for them, and re-layouts, on_device(): return out.transpose(2, 0, 1).reshape(rows, heads * DK)  2.27 us

profile of v5, /device:TPU:5, one launch (start us, length us, event | category | flops | bytes accessed | tf_op | source)
XLA Modules:
  0.0 27.5 jit_solution(3919331712527058622)
XLA Ops:
  0.0 25.2 %shard_map.46 = bf16[8,128,512]{2,1,0:T(8,128)(2,1)} custom-call(bf16[512,1024]{1,0:T(8,128)(2,1)} %q_hbm.1, bf16[512,1024]{1,0:T(8,128)(2,1)} %k_hbm.1, bf16[512,1024]{1,0:T(8,128)(2,1)} %v_hbm.1, f32[13,8,512]{2,1,0:T(8,128)} %w_hbm.1), custom_call_target="tpu_custom_call" | custom-call | flops 1879048192 | bytes 4194304 | tf_op jit(solution)/shard_map/pallas_call | solution.py:332
  25.3 2.3 %copy.5 = bf16[512,1024]{1,0:T(8,128)(2,1)} copy(bf16[512,1024]{0,1:T(8,128)(2,1)} %bitcast.3) | data formatting | bytes 2097152 | tf_op jit(solution)/shard_map/reshape | solution.py:368

commit v6 on v3

--- a/solution.py
+++ b/solution.py
@@ -11,7 +11,6 @@
 DK = 128
 STRETCH = 64
 SUB = 2 * STRETCH
-RELAYED = 2
 MESH = pl.DeviceIdType.MESH
 
 
@@ -32,7 +31,7 @@
     ctx_bits, grp_bits,
     q_hbm, k_hbm, v_hbm, w_hbm, out_hbm,
     q_buf, k_buf, v_buf, w_buf, w_head, vt_buf, qt_buf, sub_buf, state, sib, run, acc, out_t, out_buf,
-    in_sem, w_sem, out_sem, send_sem, fwd_sem, relay_sem, recv_sem,
+    in_sem, w_sem, out_sem, send_sem, fwd_sem, recv_sem,
 ):
     heads, rows = q_buf.shape[0], q_buf.shape[1]
     half = heads // 2
@@ -49,12 +48,8 @@
             return (ctx // 2**j) % 2
         return (grp // 2 ** (j - ctx_bits)) % 2
 
-    inner = (bit(1) + bit(2)) % 2
-
     def partner(j):
         step = 1 - 2 * bit(j)
-        if j == RELAYED:
-            return (grp, ctx + step * 2)
         if j < ctx_bits:
             return (grp, ctx + step * 2**j)
         return (grp + step * 2 ** (j - ctx_bits), ctx)
@@ -93,10 +88,6 @@
     def forward(j, i):
         h = mine(i)
         return remote(sib.at[j, h], j, h, fwd_sem.at[j, h], partner(0))
-
-    def relay(i):
-        h = mine(i)
-        return remote(sib.at[RELAYED, h], RELAYED, h, relay_sem.at[h], partner(1))
 
     def arrival(j, h):
         return remote(sib.at[j, h], j, h, send_sem.at[j, h], partner(0))
@@ -111,14 +102,7 @@
             fetch(2, h).start()
         if i == 0:
             for j in range(depth):
-                if j == RELAYED:
-                    @pl.when(inner == 1)
-                    def _():
-                        pl.semaphore_signal(
-                            barrier, inc=1, device_id=partner(j), device_id_type=MESH
-                        )
-                else:
-                    pl.semaphore_signal(barrier, inc=1, device_id=partner(j), device_id_type=MESH)
+                pl.semaphore_signal(barrier, inc=1, device_id=partner(j), device_id_type=MESH)
     fetch_w().start()
     for i in range(half):
         for h in (mine(i), other(i)):
@@ -209,15 +193,11 @@
             pl.when(condition)(action)
 
     def sends(j):
-        if j == RELAYED:
-            return inner == 1
         return bit(j) == 0 if j == last else None
 
     def receive(j, i):
         h = mine(i)
         guarded(bit(j) == 1 if j == last else None, lambda: arrival(j, h).wait_recv())
-        if j == RELAYED:
-            guarded(inner == 1, lambda: relay(i).start())
         if j >= 1:
             guarded(bit(j) == 1, lambda: forward(j, i).start())
         if j < last:
@@ -230,7 +210,7 @@
 
     block_sum(other(0))
     block_sum(mine(0))
-    pl.semaphore_wait(barrier, depth - 1 + inner)
+    pl.semaphore_wait(barrier, depth)
     first_sends(0)
 
     def open_pair(i, carry):
@@ -299,8 +279,6 @@
         for j in range(1, depth):
             guarded(sends(j), lambda: stage_send(j, i).wait_send())
             guarded(bit(j) == 1, lambda: forward(j, i).wait_send())
-            if j == RELAYED:
-                guarded(inner == 1, lambda: relay(i).wait_send())
         return carry
 
     lax.fori_loop(0, half, close, 0)
@@ -341,7 +319,6 @@
             pltpu.SemaphoreType.DMA((heads,)),
             pltpu.SemaphoreType.DMA((depth, heads)),
             pltpu.SemaphoreType.DMA((depth, heads)),
-            pltpu.SemaphoreType.DMA((heads,)),
             pltpu.SemaphoreType.DMA((depth, heads)),
         ],
         compiler_params=pltpu.CompilerParams(

time: 27.1 us -> 27.2 us (level)
  no operation moved by 1% of the time
where the time goes in v6:
time: 27.2 us; the launch traced here: 27 us
  Pallas kernels  24.7 us (91%)
  local copies, waits for them, and re-layouts  2.27 us (8%)
    pallas_call x1, Pallas kernels, on_device(): pl.pallas_call(functools.partial(kernel, ctx_bits, grp_bits), out_shape=j...  24.7 us
    reshape x1, local copies, waits for them, and re-layouts, on_device(): return out.transpose(2, 0, 1).reshape(rows, heads * DK)  2.27 us

profile of v6, /device:TPU:5, one launch (start us, length us, event | category | flops | bytes accessed | tf_op | source)
XLA Modules:
  0.0 27.0 jit_solution(13180187021356936935)
XLA Ops:
  0.0 24.7 %shard_map.46 = bf16[8,128,512]{2,1,0:T(8,128)(2,1)} custom-call(bf16[512,1024]{1,0:T(8,128)(2,1)} %q_hbm.1, bf16[512,1024]{1,0:T(8,128)(2,1)} %k_hbm.1, bf16[512,1024]{1,0:T(8,128)(2,1)} %v_hbm.1, f32[13,8,512]{2,1,0:T(8,128)} %w_hbm.1), custom_call_target="tpu_custom_call" | custom-call | flops 1879048192 | bytes 4194304 | tf_op jit(solution)/shard_map/pallas_call | solution.py:297
  24.7 2.3 %copy.5 = bf16[512,1024]{1,0:T(8,128)(2,1)} copy(bf16[512,1024]{0,1:T(8,128)(2,1)} %bitcast.3) | data formatting | bytes 2097152 | tf_op jit(solution)/shard_map/reshape | solution.py:332

commit v7 on v6

--- a/solution.py
+++ b/solution.py
@@ -322,7 +322,7 @@
             pltpu.SemaphoreType.DMA((depth, heads)),
         ],
         compiler_params=pltpu.CompilerParams(
-            collective_id=0, has_side_effects=True, vmem_limit_bytes=60 * 2**20
+            collective_id=0, has_side_effects=True, vmem_limit_bytes=52 * 2**20
         ),
         cost_estimate=pl.CostEstimate(
             flops=2 * rows * heads * DK * DK * (9 + depth), bytes_accessed=8 * rows * heads * DK,

time: 27.2 us -> 27.6 us (1.015)
  Pallas kernels: 24.7 us -> 25.2 us
    reshape x1, local copies, waits for them, and re-layouts: 2.27 us -> 1.32 us  [on_device(): return out.transpose(2, 0, 1).reshape(rows, heads * DK)]
    unnamed x0 -> x2, local copies, waits for them, and re-layouts: none -> 0.93 us
    pallas_call x1, Pallas kernels: 24.7 us -> 25.2 us  [on_device(): pl.pallas_call(functools.partial(kernel, ctx_bits, grp_bits), out_shape=j...]
where the time goes in v7:
time: 27.6 us; the launch traced here: 27.5 us
  Pallas kernels  25.2 us (91%)
  local copies, waits for them, and re-layouts  2.25 us (8%)
    pallas_call x1, Pallas kernels, on_device(): pl.pallas_call(functools.partial(kernel, ctx_bits, grp_bits), out_shape=j...  25.2 us
    reshape x1, local copies, waits for them, and re-layouts, on_device(): return out.transpose(2, 0, 1).reshape(rows, heads * DK)  1.32 us
    unnamed x2, local copies, waits for them, and re-layouts  0.93 us

profile of v7, /device:TPU:5, one launch (start us, length us, event | category | flops | bytes accessed | tf_op | source)
XLA Modules:
  0.0 27.5 jit_solution(7931650483509385351)
XLA Ops:
  0.0 0.0 copy-start
  0.0 0.9 %copy-done = f32[13,8,512]{2,1,0:T(8,128)S(1)} copy-done((f32[13,8,512]{2,1,0:T(8,128)S(1)}, f32[13,8,512]{2,1,0:T(8,128)}, u32[]{:S(2)}) %copy-start) | copy-done | bytes 213016
  0.9 25.2 %shard_map.46 = bf16[8,128,512]{2,1,0:T(8,128)(2,1)S(1)} custom-call(bf16[512,1024]{1,0:T(8,128)(2,1)} %q_hbm.1, bf16[512,1024]{1,0:T(8,128)(2,1)} %k_hbm.1, bf16[512,1024]{1,0:T(8,128)(2,1)} %v_hbm.1, f32[13,8,512]{2,1,0:T(8,128)S(1)} %copy-done), custom_call_target="tpu_custom_call" | custom-call | flops 1879048192 | bytes 4194304 | tf_op jit(solution)/shard_map/pallas_call | solution.py:297
  26.1 1.3 %copy.5 = bf16[512,1024]{1,0:T(8,128)(2,1)} copy(bf16[512,1024]{0,1:T(8,128)(2,1)S(1)} %bitcast.3) | data formatting | bytes 2097152 | tf_op jit(solution)/shard_map/reshape | solution.py:332
Async XLA Ops:
  0.0 0.9 %copy-start = (f32[13,8,512]{2,1,0:T(8,128)S(1)}, f32[13,8,512]{2,1,0:T(8,128)}, u32[]{:S(2)}) copy-start(f32[13,8,512]{2,1,0:T(8,128)} %w_hbm.1) | copy-start | bytes 638980

commit v8 on v6

--- a/solution.py
+++ b/solution.py
@@ -221,14 +221,14 @@
         return carry
 
     lax.fori_loop(1, half, open_pair, 0)
-    receive(0, half - 1)
     fetch_w().wait()
     for level in range(1 + local_bits + depth):
         for h in range(heads):
             w_head[h, level : level + 1, :] = w_buf[level, h : h + 1, :] * level_factor(level)
 
-    lag = [0, 1, half] + [2 * half + 2 * j for j in range(depth - 3)]
-    lag_middle = max(2 * half, lag[ctx_bits - 1] + 1)
+    receive(0, half - 1)
+    lag = [0] + [1 + 2 * j for j in range(depth - 1)]
+    lag_middle = max(half + 2, lag[ctx_bits - 1] + 1)
 
     def between(i, low, high):
         return jnp.logical_and(i >= low, i < high)

time: 27.2 us -> 27.7 us (1.018)
  Pallas kernels: 24.7 us -> 25.3 us
    pallas_call x1, Pallas kernels: 24.7 us -> 25.3 us  [on_device(): pl.pallas_call(functools.partial(kernel, ctx_bits, grp_bits), out_shape=j...]
where the time goes in v8:
time: 27.7 us; the launch traced here: 27.6 us
  Pallas kernels  25.3 us (91%)
  local copies, waits for them, and re-layouts  2.27 us (8%)
    pallas_call x1, Pallas kernels, on_device(): pl.pallas_call(functools.partial(kernel, ctx_bits, grp_bits), out_shape=j...  25.3 us
    reshape x1, local copies, waits for them, and re-layouts, on_device(): return out.transpose(2, 0, 1).reshape(rows, heads * DK)  2.27 us

profile of v8, /device:TPU:5, one launch (start us, length us, event | category | flops | bytes accessed | tf_op | source)
XLA Modules:
  0.0 27.6 jit_solution(2396606394410476713)
XLA Ops:
  0.0 25.3 %shard_map.46 = bf16[8,128,512]{2,1,0:T(8,128)(2,1)} custom-call(bf16[512,1024]{1,0:T(8,128)(2,1)} %q_hbm.1, bf16[512,1024]{1,0:T(8,128)(2,1)} %k_hbm.1, bf16[512,1024]{1,0:T(8,128)(2,1)} %v_hbm.1, f32[13,8,512]{2,1,0:T(8,128)} %w_hbm.1), custom_call_target="tpu_custom_call" | custom-call | flops 1879048192 | bytes 4194304 | tf_op jit(solution)/shard_map/pallas_call | solution.py:297
  25.3 2.3 %copy.5 = bf16[512,1024]{1,0:T(8,128)(2,1)} copy(bf16[512,1024]{0,1:T(8,128)(2,1)} %bitcast.3) | data formatting | bytes 2097152 | tf_op jit(solution)/shard_map/reshape | solution.py:332
